TPU v7x, 256 devices: a whole 4x4x8 slice. The times are simulated.
256 devices in a mesh: noise: 8 (over x, core), dp: 32 (over y, z).
Axes of the slice: x: 4, y: 4, z: 8, core: 2. Of those that a mesh axis runs over, the one named last changes fastest.
Arguments:
- noise_latents: bfloat16 [8192, 1024], P('noise', 'dp'), may hold values from -8 to 8
- data_latents: bfloat16 [32768, 1024], P('dp', 'noise'), may hold values from -8 to 8
Outputs:
- targets: float32 [8192, 1024], P('noise', 'dp')
- row_potential: float32 [8192], P('noise')
- col_potential: float32 [32768], P('dp')
All inputs are finite; a program needn't handle non-finite values.
Results may differ from a plain program's by a relative error of at most 0.0027.
Values may be sent and summed in bfloat16 or wider, within the bound.
A program may use at most 64 MiB of HBM per device.

v0:
```python
import jax
import jax.numpy as jnp
from jax import lax
from jax.sharding import PartitionSpec as P

D = 1024
ITERS = 3


epsilon_value = 0.05


def row_logsum(logits):
    largest = lax.pmax(jnp.max(logits, axis=1), "dp")
    summed = lax.psum(jnp.sum(jnp.exp(logits - largest[:, None]), axis=1), "dp")
    return largest + jnp.log(summed)


def col_logsum(logits):
    largest = lax.pmax(jnp.max(logits, axis=0), "noise")
    summed = lax.psum(jnp.sum(jnp.exp(logits - largest[None, :]), axis=0), "noise")
    return largest + jnp.log(summed)


def body(noise_latents, data_latents):
    noise_full = lax.all_gather(noise_latents, "dp", axis=1, tiled=True)
    data_full = lax.all_gather(data_latents, "noise", axis=1, tiled=True)
    noise_norms = jnp.sum(jnp.square(noise_full.astype(jnp.float32)), axis=1)
    data_norms = jnp.sum(jnp.square(data_full.astype(jnp.float32)), axis=1)
    inner = lax.dot_general(
        noise_full, data_full, (((1,), (1,)), ((), ())), preferred_element_type=jnp.float32
    )
    distance = (noise_norms[:, None] + data_norms[None, :] - 2.0 * inner) / D
    rows_here = noise_full.shape[0]
    cols_here = data_full.shape[0]
    total_rows = rows_here * lax.axis_size("noise")
    total_cols = cols_here * lax.axis_size("dp")
    log_rows = jnp.log(jnp.float32(total_rows))
    log_cols = jnp.log(jnp.float32(total_cols))

    def row_update(col_potential):
        logits = (col_potential[None, :] - distance) / epsilon_value
        return -epsilon_value * (row_logsum(logits) - log_cols)

    col_potential = jnp.zeros((cols_here,), jnp.float32)
    for number in range(ITERS):
        row_potential = row_update(col_potential)
        logits = (row_potential[:, None] - distance) / epsilon_value
        col_potential = -epsilon_value * (col_logsum(logits) - log_rows)
    row_potential = row_update(col_potential)
    weights = (
        jnp.exp((row_potential[:, None] + col_potential[None, :] - distance) / epsilon_value)
        / total_cols
    ).astype(jnp.bfloat16)
    width = D // lax.axis_size("dp")
    partial_value = jnp.dot(weights, data_full, preferred_element_type=jnp.float32)
    summed = lax.psum(partial_value, "dp")
    targets = lax.dynamic_slice_in_dim(summed, lax.axis_index("dp") * width, width, 1)
    return (targets, row_potential, col_potential)


def solution(mesh):
    return jax.shard_map(
        body,
        mesh=mesh,
        in_specs=(P("noise", "dp"), P("dp", "noise")),
        out_specs=(P("noise", "dp"), P("noise"), P("dp")),
        check_vma=False,
    )
```

profile of v0, /device:TPU:4, one launch (start us, length us, event | category | flops | bytes accessed | tf_op | source)
XLA Modules:
  0.0 982.8 jit_solution(17625296369418744678)
XLA Ops:
  8.7 33.6 %all-gather.5.cloned.1.call-done = bf16[1024,1024]{1,0:T(8,128)(2,1)} async-done(((bf16[1024,128]{1,0:T(8,128)(2,1)}), bf16[1024,1024]{1,0:T(8,128)(2,1)}) %all-gather.5.cloned.1.call-update) | async-done | bytes 2097168 | tf_op jit(solution)/shard_map/all_gather | solution.py:27
  44.5 79.6 %all-gather.3.cloned.1.call-done = bf16[1024,1024]{0,1:T(8,128)(2,1)} async-done(((bf16[1024,32]{0,1:T(8,128)(2,1)}), bf16[1024,1024]{0,1:T(8,128)(2,1)}) %all-gather.3.cloned.1.call-update) | async-done | bytes 2097168 | tf_op jit(solution)/shard_map/all_gather | solution.py:26
  126.2 6.2 fusion
  132.4 72.1 %pmax.49 = f32[1024]{0:T(1024)S(1)} all-reduce(f32[1024]{0:T(1024)S(1)} %get-tuple-element.3), channel_id=1, replica_groups=mesh['noise'=8,'dp'=32] {'dp'}, use_global_device_ids=true, to_apply=%region_3.0 | all-reduce | flops 1024 | bytes 8192 | tf_op jit(solution)/shard_map/pmax | solution.py:14
  207.6 69.6 %psum.56 = f32[1024]{0:T(1024)S(1)} all-reduce(f32[1024]{0:T(1024)S(1)} %exponential_reduce_fusion.6), channel_id=1, replica_groups=mesh['noise'=8,'dp'=32] {'dp'}, use_global_device_ids=true, to_apply=%region_5.0 | all-reduce | flops 1024 | bytes 8192 | tf_op jit(solution)/shard_map/psum | solution.py:15
  279.9 10.3 %pmax.50 = f32[1024]{0:T(1024)S(1)} all-reduce(f32[1024]{0:T(1024)S(1)} %fusion.1), channel_id=1, replica_groups=mesh['noise'=8,'dp'=32] {'noise'}, use_global_device_ids=true, to_apply=%region_7.0 | all-reduce | flops 1024 | bytes 8192 | tf_op jit(solution)/shard_map/pmax | solution.py:20
  290.1 3.2 exponential_reduce_fusion.5
  293.3 10.4 %psum.57 = f32[1024]{0:T(1024)S(1)} all-reduce(f32[1024]{0:T(1024)S(1)} %exponential_reduce_fusion.5), channel_id=1, replica_groups=mesh['noise'=8,'dp'=32] {'noise'}, use_global_device_ids=true, to_apply=%region_9.0 | all-reduce | flops 1024 | bytes 8192 | tf_op jit(solution)/shard_map/psum | solution.py:21
  306.4 71.7 %pmax.51 = f32[1024]{0:T(1024)S(1)} all-reduce(f32[1024]{0:T(1024)S(1)} %fusion.2), channel_id=1, replica_groups=mesh['noise'=8,'dp'=32] {'dp'}, use_global_device_ids=true, to_apply=%region_11.0 | all-reduce | flops 1024 | bytes 8192 | tf_op jit(solution)/shard_map/pmax | solution.py:14
  378.0 3.1 exponential_reduce_fusion.4
  381.1 69.6 %psum.58 = f32[1024]{0:T(1024)S(1)} all-reduce(f32[1024]{0:T(1024)S(1)} %exponential_reduce_fusion.4), channel_id=1, replica_groups=mesh['noise'=8,'dp'=32] {'dp'}, use_global_device_ids=true, to_apply=%region_13.0 | all-reduce | flops 1024 | bytes 8192 | tf_op jit(solution)/shard_map/psum | solution.py:15
  453.4 10.8 %pmax.52 = f32[1024]{0:T(1024)S(1)} all-reduce(f32[1024]{0:T(1024)S(1)} %fusion.3), channel_id=1, replica_groups=mesh['noise'=8,'dp'=32] {'noise'}, use_global_device_ids=true, to_apply=%region_15.0 | all-reduce | flops 1024 | bytes 8192 | tf_op jit(solution)/shard_map/pmax | solution.py:20
  464.3 3.2 exponential_reduce_fusion.3
  467.4 14.0 %psum.59 = f32[1024]{0:T(1024)S(1)} all-reduce(f32[1024]{0:T(1024)S(1)} %exponential_reduce_fusion.3), channel_id=1, replica_groups=mesh['noise'=8,'dp'=32] {'noise'}, use_global_device_ids=true, to_apply=%region_17.0 | all-reduce | flops 1024 | bytes 8192 | tf_op jit(solution)/shard_map/psum | solution.py:21
  484.1 71.6 %pmax.53 = f32[1024]{0:T(1024)S(1)} all-reduce(f32[1024]{0:T(1024)S(1)} %fusion.4), channel_id=1, replica_groups=mesh['noise'=8,'dp'=32] {'dp'}, use_global_device_ids=true, to_apply=%region_19.0 | all-reduce | flops 1024 | bytes 8192 | tf_op jit(solution)/shard_map/pmax | solution.py:14
  558.8 69.6 %psum.60 = f32[1024]{0:T(1024)S(1)} all-reduce(f32[1024]{0:T(1024)S(1)} %exponential_reduce_fusion.2), channel_id=1, replica_groups=mesh['noise'=8,'dp'=32] {'dp'}, use_global_device_ids=true, to_apply=%region_21.0 | all-reduce | flops 1024 | bytes 8192 | tf_op jit(solution)/shard_map/psum | solution.py:15
  631.2 11.0 %pmax.54 = f32[1024]{0:T(1024)S(1)} all-reduce(f32[1024]{0:T(1024)S(1)} %fusion.5), channel_id=1, replica_groups=mesh['noise'=8,'dp'=32] {'noise'}, use_global_device_ids=true, to_apply=%region_23.0 | all-reduce | flops 1024 | bytes 8192 | tf_op jit(solution)/shard_map/pmax | solution.py:20
  642.2 3.2 exponential_reduce_fusion.1
  645.3 14.0 %psum.61 = f32[1024]{0:T(1024)S(1)} all-reduce(f32[1024]{0:T(1024)S(1)} %exponential_reduce_fusion.1), channel_id=1, replica_groups=mesh['noise'=8,'dp'=32] {'noise'}, use_global_device_ids=true, to_apply=%region_25.0 | all-reduce | flops 1024 | bytes 8192 | tf_op jit(solution)/shard_map/psum | solution.py:21
  662.0 71.6 %pmax.55 = f32[1024]{0:T(1024)S(1)} all-reduce(f32[1024]{0:T(1024)S(1)} %fusion.6), channel_id=1, replica_groups=mesh['noise'=8,'dp'=32] {'dp'}, use_global_device_ids=true, to_apply=%region_27.0 | all-reduce | flops 1024 | bytes 8192 | tf_op jit(solution)/shard_map/pmax | solution.py:14
  733.7 3.1 exponential_reduce_fusion
  736.8 69.6 %psum.62 = f32[1024]{0:T(1024)S(1)} all-reduce(f32[1024]{0:T(1024)S(1)} %exponential_reduce_fusion), channel_id=1, replica_groups=mesh['noise'=8,'dp'=32] {'dp'}, use_global_device_ids=true, to_apply=%region_29.0 | all-reduce | flops 1024 | bytes 8192 | tf_op jit(solution)/shard_map/psum | solution.py:15
  806.4 6.9 fusion.7
  813.3 161.3 %all-reduce.2.cloned.1.call-done = f32[1024,1024]{0,1:T(8,128)} async-done(((f32[1024,1024]{0,1:T(8,128)}), f32[1024,1024]{0,1:T(8,128)}) %all-reduce.2.cloned.1.call-update) | async-done | bytes 4194320 | tf_op jit(solution)/shard_map/psum | solution.py:57
  (30 shorter events, 29.6 us)
Async XLA Ops:
  7.2 35.1 %all-gather.5.cloned.1.call-start = ((), (), s32[]{:S(2)}) async-start(), calls=%async_computation.1 | async-start | bytes 2359296 | tf_op jit(solution)/shard_map/all_gather | solution.py:27
  7.9 116.2 %all-gather.3.cloned.1.call-start = ((), (), s32[]{:S(2)}) async-start(), calls=%async_computation | async-start | bytes 2162688 | tf_op jit(solution)/shard_map/all_gather | solution.py:26
  8.6 966.0 %all-reduce.2.cloned.1.call-start = ((), (), s32[]{:S(2)}) async-start(), calls=%async_computation.2 | async-start | bytes 8388608 | tf_op jit(solution)/shard_map/psum | solution.py:57
  42.3 83.9 %copy-start = (bf16[1024,1024]{1,0:T(8,128)(2,1)S(1)}, bf16[1024,1024]{1,0:T(8,128)(2,1)}, u32[]{:S(2)}) copy-start(bf16[1024,1024]{1,0:T(8,128)(2,1)} %all-gather.5.cloned.1.call-done) | copy-start | bytes 6291460
  659.4 147.1 %copy-start.1 = (f32[1024]{0:T(1024)}, f32[1024]{0:T(1024)S(1)}, u32[]{:S(2)}) copy-start(f32[1024]{0:T(1024)S(1)} %add_multiply_fusion.1) | copy-start | bytes 12292
  806.4 6.9 copy-start.2
Sparse Core Ops, SparseCore 0:
  9.8 32.4 all-gather.4
  44.9 79.2 all-gather.2
  813.5 161.1 all-reduce.1
where the time goes:
time: 984 us; the launch traced here: 983 us
  blocking collectives  636 us (65%)
  waiting for transfers between devices  276 us (28%)
  other arithmetic  42.2 us (4%)
  between operations  13.9 us (1%)
  matrix products  13.1 us (1%)
    pmax x4, blocking collectives, row_logsum(): largest = lax.pmax(jnp.max(logits, axis=1), 'dp')  287 us
    psum x4, blocking collectives, row_logsum(): summed = lax.psum(jnp.sum(jnp.exp(logits - largest[:, None]), axis=1), 'dp')  279 us
    psum x1, waiting for transfers between devices, body(): summed = lax.psum(partial_value, 'dp')  161 us
    all_gather x1, waiting for transfers between devices, body(): noise_full = lax.all_gather(noise_latents, 'dp', axis=1, tiled=True)  79.6 us
    psum x3, blocking collectives, col_logsum(): lax.psum(jnp.sum(jnp.exp(logits - largest[None, :]), axis=0), 'noise')  38.4 us
    all_gather x1, waiting for transfers between devices, body(): data_full = lax.all_gather(data_latents, 'noise', axis=1, tiled=True)  33.6 us
    pmax x3, blocking collectives, col_logsum(): largest = lax.pmax(jnp.max(logits, axis=0), 'noise')  32.1 us
  transfers between devices with their start and end apart: 3, of which 3 were waited for; matrix products, arithmetic and copies ran while one was open for 0% of the time, Pallas kernels for 0%

commit v1 on v0

v1 whole, which is shorter than its diff:
```python
import math

import jax
import jax.numpy as jnp
from jax import lax
from jax.experimental import pallas as pl
from jax.experimental.pallas import tpu as pltpu
from jax.sharding import PartitionSpec as P

D = 1024
ITERS = 3
EPS = 0.05
ROWS = 1024
COLS = 1024
NX, NY, NZ = 4, 4, 8
WIDTH = D // (NY * NZ)
DEPTH = D // (2 * NX)
F32, BF16 = jnp.float32, jnp.bfloat16
MESH = pl.DeviceIdType.MESH

LOG2E = math.log2(math.e)
TO_LOGIT = 2.0 * LOG2E / (D * EPS)
NORM_LOGIT = LOG2E / (D * EPS)
TO_POTENTIAL = EPS / LOG2E

GATHER_ZY = 768
SUM_ZY = 256


def hops(by):
    dy, dz = by
    return min(dy, NY - dy) + min(dz, NZ - dz)


DP_PEERS = sorted(
    ((dy, dz) for dy in range(NY) for dz in range(NZ) if dy or dz), key=lambda by: -hops(by)
)
NOISE_PEERS = [(2, 1), (2, 0), (1, 1), (3, 1), (1, 0), (3, 0), (0, 1)]
Z_NEAR = [1, 7, 2, 6, 3, 5, 4]
Z_FAR = [4, 3, 5, 2, 6, 1, 7]
Y_FAR = [2, 1, 3]
Y_NEAR = [1, 3, 2]


def rows_at(start, size):
    return pl.ds(pl.multiple_of(start, size), size)


def diagonal():
    sub = lax.broadcasted_iota(jnp.int32, (8, 128), 0)
    lane = lax.broadcasted_iota(jnp.int32, (8, 128), 1)
    return lane - sub


def spread(packed, wide):
    for a in range(8):
        wide[pl.ds(128 * a, 128), :] = jnp.broadcast_to(packed[a : a + 1, :], (128, 128)).T


def row_logsum(logit, wide, out, weights=None):
    def first(t, acc):
        r = rows_at(8 * t, 8)
        g = wide[r, :]
        return tuple(jnp.maximum(acc[c], logit[r, 128 * c : 128 * c + 128] + g) for c in range(8))

    low = tuple(jnp.full((8, 128), -jnp.inf, F32) for _ in range(8))
    acc = lax.fori_loop(0, COLS // 8, first, low, unroll=8)
    top = [jnp.broadcast_to(jnp.max(a, axis=0, keepdims=True), (8, 128)) for a in acc]
    zero = tuple(jnp.zeros((8, 128), F32) for _ in range(8))

    def second(t, acc):
        r = rows_at(8 * t, 8)
        g = wide[r, :]
        return tuple(
            acc[c] + jnp.exp2(logit[r, 128 * c : 128 * c + 128] + g - top[c]) for c in range(8)
        )

    def second_kept(t, acc):
        r = rows_at(16 * t, 16)
        g = wide[r, :]
        sums = []
        for c in range(8):
            both = jnp.concatenate([top[c], top[c]], axis=0)
            e = jnp.exp2(logit[r, 128 * c : 128 * c + 128] + g - both)
            weights[r, 128 * c : 128 * c + 128] = e.astype(BF16)
            sums.append(acc[c] + e[:8] + e[8:])
        return tuple(sums)

    if weights is None:
        acc = lax.fori_loop(0, COLS // 8, second, zero, unroll=8)
    else:
        acc = lax.fori_loop(0, COLS // 16, second_kept, zero, unroll=4)
    for c in range(8):
        out[c : c + 1, :] = top[c][:1] + jnp.log2(jnp.sum(acc[c], axis=0, keepdims=True))
    return top


def col_logsum(logit, packed, out):
    f = [jnp.broadcast_to(packed[c : c + 1, :], (8, 128)) for c in range(8)]
    off = diagonal()

    def block(a, _):
        acc = jnp.zeros((8, 128), F32)
        for b in range(16):
            r = rows_at(128 * a + 8 * b, 8)
            v = [logit[r, 128 * c : 128 * c + 128] + f[c] for c in range(8)]
            m = jnp.maximum(
                jnp.maximum(jnp.maximum(v[0], v[1]), jnp.maximum(v[2], v[3])),
                jnp.maximum(jnp.maximum(v[4], v[5]), jnp.maximum(v[6], v[7])),
            )
            m = jnp.max(m, axis=1, keepdims=True)
            e = [jnp.exp2(x - m) for x in v]
            s = ((e[0] + e[1]) + (e[2] + e[3])) + ((e[4] + e[5]) + (e[6] + e[7]))
            s = jnp.sum(s, axis=1, keepdims=True)
            acc = jnp.where(off == 8 * b, jnp.broadcast_to(m + jnp.log2(s), (8, 128)), acc)
        out[pl.ds(a, 1), :] = jnp.sum(acc, axis=0, keepdims=True)
        return 0

    lax.fori_loop(0, 8, block, 0)


def combine(parts, count):
    values = [parts[k] for k in range(count)]
    top = values[0]
    for v in values[1:]:
        top = jnp.maximum(top, v)
    total = jnp.exp2(values[0] - top)
    for v in values[1:]:
        total = total + jnp.exp2(v - top)
    return top + jnp.log2(total)


def norms(source, out):
    def step(t, acc):
        v = source[rows_at(16 * t, 16), :].astype(F32)
        v = v * v
        return acc + v[:8] + v[8:]

    acc = lax.fori_loop(0, D // 16, step, jnp.zeros((8, 1024), F32), unroll=2)
    s = jnp.sum(acc, axis=0, keepdims=True)
    for c in range(8):
        out[c : c + 1, :] = s[:, 128 * c : 128 * c + 128]


def kernel(
    noise_ref, data_ref, targets_ref, row_ref, col_ref,
    noise_full, data_full, data_t, logit, weights, partial, partial_half,
    wide, noise_norm, data_norm, f_packed, g_packed,
    row_parts, col_parts, sum_yz1, sum_yz2, sum_zy1, sum_zy2, send_yz2, send_zy2,
    own_sem, data_send, data_recv, pair_send, pair_recv,
    zy1_send, zy1_recv, zy2_send, zy2_recv, yz1_send, yz1_recv, yz2_send, yz2_recv,
    row_send, row_recv, col_send, col_recv,
    a1_send, a1_recv, a2_send, a2_recv, b1_send, b1_recv, b2_send, b2_recv,
):
    n = lax.axis_index("noise")
    k = lax.axis_index("dp")
    xs = [lax.rem(lax.div(n, 2) + d, NX) for d in range(NX)]
    cores = [lax.rem(n + d, 2) for d in range(2)]
    ys = [lax.rem(lax.div(k, NZ) + d, NY) for d in range(NY)]
    zs = [lax.rem(k + d, NZ) for d in range(NZ)]

    def dp_peer(dy, dz):
        return (n, ys[dy] * NZ + zs[dz])

    def noise_peer(dx, dc):
        return (xs[dx] * 2 + cores[dc], k)

    def remote(src, dst, send, recv, peer):
        copy = pltpu.make_async_remote_copy(
            src_ref=src, dst_ref=dst, send_sem=send, recv_sem=recv,
            device_id=peer, device_id_type=MESH,
        )
        copy.start()

    def wait_for(ref, sem):
        pltpu.make_async_copy(ref, ref, sem).wait()

    barrier = pltpu.get_barrier_semaphore()
    peers = [dp_peer(*by) for by in DP_PEERS] + [noise_peer(*by) for by in NOISE_PEERS]
    for peer in peers:
        pl.semaphore_signal(barrier, inc=1, device_id=peer, device_id_type=MESH)
    pl.semaphore_wait(barrier, len(peers))

    lanes_a, lanes_b = pl.ds(0, GATHER_ZY), pl.ds(GATHER_ZY, ROWS - GATHER_ZY)

    def noise_block(dy, dz, lanes):
        return noise_full.at[rows_at((ys[dy % NY] * NZ + zs[dz % NZ]) * WIDTH, WIDTH), lanes]

    def data_block(dx, dc):
        return data_full.at[:, rows_at((xs[dx % NX] * 2 + cores[dc]) * DEPTH, DEPTH)]

    own_noise = pltpu.make_async_copy(noise_ref, noise_block(0, 0, pl.ds(0, ROWS)), own_sem.at[0])
    own_noise.start()
    own_data = pltpu.make_async_copy(data_ref, data_block(0, 0), own_sem.at[1])
    own_data.start()
    for dz in Z_NEAR:
        remote(noise_ref.at[:, lanes_a], noise_block(0, 0, lanes_a), zy1_send, zy1_recv.at[dz], dp_peer(0, dz))
    for dy in Y_NEAR:
        remote(noise_ref.at[:, lanes_b], noise_block(0, 0, lanes_b), yz1_send, yz1_recv.at[dy], dp_peer(dy, 0))
    for dx in (1, 3, 2):
        remote(data_ref, data_block(0, 0), data_send, data_recv.at[dx], noise_peer(dx, 0))
    for dy in Y_FAR:
        remote(noise_ref.at[:, lanes_a], noise_block(0, 0, lanes_a), zy2_send, zy2_recv, dp_peer(dy, 0))
    for dz in Z_FAR:
        remote(noise_ref.at[:, lanes_b], noise_block(0, 0, lanes_b), yz2_send, yz2_recv, dp_peer(0, dz))
    remote(data_ref, data_block(0, 0), pair_send, pair_recv.at[0], noise_peer(0, 1))

    def forward_zy(dz):
        block = noise_block(0, -dz, lanes_a)
        wait_for(block, zy1_recv.at[dz])
        for dy in Y_FAR:
            remote(block, block, zy2_send, zy2_recv, dp_peer(dy, 0))

    def forward_yz(dy):
        block = noise_block(-dy, 0, lanes_b)
        wait_for(block, yz1_recv.at[dy])
        for dz in Z_FAR:
            remote(block, block, yz2_send, yz2_recv, dp_peer(0, dz))

    def forward_data(dx):
        block = data_block(-dx, 0)
        wait_for(block, data_recv.at[dx])
        remote(block, block, pair_send, pair_recv.at[dx], noise_peer(0, 1))

    forward_zy(1)
    forward_zy(7)
    forward_yz(1)
    forward_yz(3)
    forward_zy(2)
    forward_zy(6)
    forward_yz(2)
    forward_zy(3)
    forward_zy(5)
    forward_zy(4)
    forward_data(1)
    forward_data(3)
    forward_data(2)

    own_data.wait()
    for dx in range(NX):
        wait_for(data_block(-dx, 1), pair_recv.at[dx])

    def turn(t, _):
        r = rows_at(128 * t, 128)
        data_t[:, r] = data_full[r, :].T
        return 0

    lax.fori_loop(0, COLS // 128, turn, 0)
    norms(data_t, data_norm)
    g_packed[...] = data_norm[...] * (-NORM_LOGIT)
    spread(g_packed, wide)

    own_noise.wait()
    wait_for(noise_full.at[pl.ds(0, 24 * WIDTH), lanes_a], zy2_recv)
    wait_for(noise_full.at[pl.ds(0, 28 * WIDTH), lanes_b], yz2_recv)

    def product(t, _):
        r = rows_at(512 * t, 512)
        logit[r, :] = jnp.dot(data_full[r, :], noise_full[...], preferred_element_type=F32) * TO_LOGIT
        return 0

    lax.fori_loop(0, COLS // 512, product, 0)

    def send_row(t):
        own = row_parts.at[t, 31]
        for s, by in enumerate(DP_PEERS):
            remote(own, row_parts.at[t, s], row_send.at[t], row_recv.at[t], dp_peer(*by))

    def send_col(t):
        own = col_parts.at[t, 7]
        for s, by in enumerate(NOISE_PEERS):
            remote(own, col_parts.at[t, s], col_send.at[t], col_recv.at[t], noise_peer(*by))

    def iteration(t, _):
        row_logsum(logit, wide, row_parts.at[t, 31])
        send_row(t)
        wait_for(row_parts.at[t, pl.ds(0, 31)], row_recv.at[t])
        f_packed[...] = math.log2(COLS * NY * NZ) - combine(row_parts.at[t], 32)
        col_logsum(logit, f_packed, col_parts.at[t, 7])
        send_col(t)
        wait_for(col_parts.at[t, pl.ds(0, 7)], col_recv.at[t])
        g_packed[...] = math.log2(ROWS * NX * 2) - combine(col_parts.at[t], 8)
        spread(g_packed, wide)
        return 0

    lax.fori_loop(0, ITERS, iteration, 0)
    top = row_logsum(logit, wide, row_parts.at[ITERS, 31], weights)
    send_row(ITERS)

    def last_product(t, _):
        r = rows_at(256 * t, 256)
        partial[r, :] = jnp.dot(data_t[r, :], weights[...], preferred_element_type=F32)
        return 0

    lax.fori_loop(0, D // 256, last_product, 0)
    norms(noise_full, noise_norm)
    col_ref[...] = g_packed[...] * TO_POTENTIAL + data_norm[...] * (1.0 / D)
    wait_for(row_parts.at[ITERS, pl.ds(0, 31)], row_recv.at[ITERS])
    logsum = combine(row_parts.at[ITERS], 32)
    row_ref[...] = (math.log2(COLS * NY * NZ) - logsum) * TO_POTENTIAL + noise_norm[...] * (1.0 / D)
    scale = jnp.concatenate([jnp.exp2(top[c][:1] - logsum[c : c + 1, :]) for c in range(8)], axis=1)

    sum_a, sum_b = pl.ds(0, SUM_ZY), pl.ds(SUM_ZY, ROWS - SUM_ZY)
    scale_a, scale_b = scale[:, :SUM_ZY], scale[:, SUM_ZY:]

    def scaled(by, bz, lanes, factor):
        return partial[rows_at((by * NZ + bz) * WIDTH, WIDTH), lanes] * factor

    for dz in Z_FAR:
        to = zs[dz]
        for by in range(NY):
            partial_half[by, to, :, sum_a] = scaled(by, to, sum_a, scale_a).astype(BF16)
        remote(partial_half.at[:, to, :, sum_a], sum_zy1.at[dz - 1], a1_send, a1_recv, dp_peer(0, dz))
    for dz in Z_FAR + [0]:
        to = zs[dz]
        for dy in Y_FAR:
            by = ys[dy]
            partial_half[by, to, :, sum_b] = scaled(by, to, sum_b, scale_b).astype(BF16)
            remote(partial_half.at[by, to, :, sum_b], sum_yz1.at[dz, dy - 1], b1_send, b1_recv.at[dz], dp_peer(dy, 0))

    def sum_y(dz):
        wait_for(sum_yz1.at[dz], b1_recv.at[dz])
        total = scaled(ys[0], zs[dz], sum_b, scale_b)
        for s in range(NY - 1):
            total = total + sum_yz1[dz, s].astype(F32)
        return total

    for dz in Z_FAR:
        send_yz2[dz - 1] = sum_y(dz).astype(BF16)
        remote(send_yz2.at[dz - 1], sum_yz2.at[dz - 1], b2_send, b2_recv, dp_peer(0, dz))

    wait_for(sum_zy1, a1_recv)

    def sum_z(by):
        total = scaled(by, zs[0], sum_a, scale_a)
        for s in range(NZ - 1):
            total = total + sum_zy1[s, by].astype(F32)
        return total

    for dy in Y_FAR:
        send_zy2[dy - 1] = sum_z(ys[dy]).astype(BF16)
        remote(send_zy2.at[dy - 1], sum_zy2.at[dy - 1], a2_send, a2_recv, dp_peer(dy, 0))

    total_a = sum_z(ys[0])
    total_b = sum_y(0)
    wait_for(sum_zy2, a2_recv)
    for s in range(NY - 1):
        total_a = total_a + sum_zy2[s].astype(F32)
    targets_ref[:, sum_a] = total_a
    wait_for(sum_yz2, b2_recv)
    for s in range(NZ - 1):
        total_b = total_b + sum_yz2[s].astype(F32)
    targets_ref[:, sum_b] = total_b

    wait_for(noise_full.at[pl.ds(0, 7 * WIDTH), lanes_a], zy1_send)
    wait_for(noise_full.at[pl.ds(0, 24 * WIDTH), lanes_a], zy2_send)
    wait_for(noise_full.at[pl.ds(0, 3 * WIDTH), lanes_b], yz1_send)
    wait_for(noise_full.at[pl.ds(0, 28 * WIDTH), lanes_b], yz2_send)
    wait_for(data_full.at[:, pl.ds(0, 3 * DEPTH)], data_send)
    wait_for(data_full.at[:, pl.ds(0, 4 * DEPTH)], pair_send)
    for t in range(ITERS + 1):
        wait_for(row_parts.at[t, pl.ds(0, 31)], row_send.at[t])
    for t in range(ITERS):
        wait_for(col_parts.at[t, pl.ds(0, 7)], col_send.at[t])
    wait_for(sum_zy1, a1_send)
    wait_for(sum_zy2, a2_send)
    wait_for(sum_yz1, b1_send)
    wait_for(sum_yz2, b2_send)


def body(noise_latents, data_latents):
    dma = pltpu.SemaphoreType.DMA
    rest = ROWS - SUM_ZY
    targets, row_potential, col_potential = pl.pallas_call(
        kernel,
        out_shape=(
            jax.ShapeDtypeStruct((WIDTH, ROWS), F32),
            jax.ShapeDtypeStruct((8, 128), F32),
            jax.ShapeDtypeStruct((8, 128), F32),
        ),
        in_specs=[pl.BlockSpec(memory_space=pl.ANY)] * 2,
        out_specs=[pl.BlockSpec(memory_space=pltpu.VMEM)] * 3,
        scratch_shapes=[
            pltpu.VMEM((D, ROWS), BF16),
            pltpu.VMEM((COLS, D), BF16),
            pltpu.VMEM((D, COLS), BF16),
            pltpu.VMEM((COLS, ROWS), F32),
            pltpu.VMEM((COLS, ROWS), BF16),
            pltpu.VMEM((D, ROWS), F32),
            pltpu.VMEM((NY, NZ, WIDTH, ROWS), BF16),
            pltpu.VMEM((COLS, 128), F32),
            pltpu.VMEM((8, 128), F32),
            pltpu.VMEM((8, 128), F32),
            pltpu.VMEM((8, 128), F32),
            pltpu.VMEM((8, 128), F32),
            pltpu.VMEM((ITERS + 1, 32, 8, 128), F32),
            pltpu.VMEM((ITERS, 8, 8, 128), F32),
            pltpu.VMEM((NZ, NY - 1, WIDTH, rest), BF16),
            pltpu.VMEM((NZ - 1, WIDTH, rest), BF16),
            pltpu.VMEM((NZ - 1, NY, WIDTH, SUM_ZY), BF16),
            pltpu.VMEM((NY - 1, WIDTH, SUM_ZY), BF16),
            pltpu.VMEM((NZ - 1, WIDTH, rest), BF16),
            pltpu.VMEM((NY - 1, WIDTH, SUM_ZY), BF16),
            dma((2,)),
            dma, dma((NX,)), dma, dma((NX,)),
            dma, dma((NZ,)), dma, dma,
            dma, dma((NY,)), dma, dma,
            dma((ITERS + 1,)), dma((ITERS + 1,)), dma((ITERS,)), dma((ITERS,)),
            dma, dma, dma, dma,
            dma, dma((NZ,)), dma, dma,
        ],
        compiler_params=pltpu.CompilerParams(
            collective_id=0, has_side_effects=True, vmem_limit_bytes=48 << 20
        ),
    )(noise_latents.T, data_latents)
    return targets.T, row_potential.reshape(ROWS), col_potential.reshape(COLS)


def solution(mesh):
    return jax.shard_map(
        body,
        mesh=mesh,
        in_specs=(P("noise", "dp"), P("dp", "noise")),
        out_specs=(P("noise", "dp"), P("noise"), P("dp")),
        check_vma=False,
    )
```

time: 984 us -> 108 us (0.11)
  blocking collectives: 636 us -> 0 us
  waiting for transfers between devices: 276 us -> 0 us
  Pallas kernels: 0 us -> 102 us
  other arithmetic: 42.2 us -> 0 us
  between operations: 13.9 us -> 0.65 us
  matrix products: 13.1 us -> 0 us
    pmax x7 -> x0, blocking collectives: 319 us -> none  [the longest x4 287 us: row_logsum(): largest = lax.pmax(jnp.max(logits, axis=1), 'dp')]
    psum x7 -> x0, blocking collectives: 317 us -> none  [the longest x4 279 us: row_logsum(): summed = lax.psum(jnp.sum(jnp.exp(logits - largest[:, None]), axis=1), 'dp')]
    psum x1 -> x0, waiting for transfers between devices: 161 us -> none  [body(): summed = lax.psum(partial_value, 'dp')]
    all_gather x2 -> x0, waiting for transfers between devices: 113 us -> none  [the longest x1 79.6 us: body(): noise_full = lax.all_gather(noise_latents, 'dp', axis=1, tiled=True)]
    pallas_call x0 -> x1, Pallas kernels: none -> 102 us  [body(): pl.pallas_call(kernel, out_shape=(jax.ShapeDtypeStruct((WIDTH, ROWS), F32...]
    reduce_sum x9 -> x0, other arithmetic: 26 us -> none  [the longest x4 12.3 us: row_logsum(): summed = lax.psum(jnp.sum(jnp.exp(logits - largest[:, None]), axis=1), 'dp')]
    reduce_max x6 -> x0, other arithmetic: 16 us -> none  [the longest x3 8.03 us: col_logsum(): largest = lax.pmax(jnp.max(logits, axis=0), 'noise')]
    dot_general x2 -> x0, matrix products: 13.1 us -> none  [the longest x1 6.88 us: body(): jnp.dot(weights, data_full, preferred_element_type=jnp.float32)]
  transfers between devices with their start and end apart: 3 -> 0, of which waited for: 3 -> 0; matrix products, arithmetic and copies ran while one was open for 0% -> 0% of each run, Pallas kernels for 0% -> 0%
where the time goes in v1:
time: 108 us; the launch traced here: 106 us
  Pallas kernels  102 us (94%)
  local copies, waits for them, and re-layouts  3.63 us (3%)
    pallas_call x1, Pallas kernels, body(): pl.pallas_call(kernel, out_shape=(jax.ShapeDtypeStruct((WIDTH, ROWS), F32...  102 us
    unnamed x7, local copies, waits for them, and re-layouts  3.63 us

profile of v1, /device:TPU:4, one launch (start us, length us, event | category | flops | bytes accessed | tf_op | source)
XLA Modules:
  0.0 106.1 jit_solution(8785648946419943722)
XLA Ops:
  0.6 0.0 copy-start
  0.6 0.9 copy-done
  1.6 0.0 copy-start.1
  1.6 0.8 copy-done.1
  2.4 101.8 %shard_map.49 = (f32[32,1024]{1,0:T(8,128)S(1)}, f32[8,128]{1,0:T(8,128)S(1)}, f32[8,128]{1,0:T(8,128)S(1)}) custom-call(bf16[32,1024]{1,0:T(8,128)(2,1)S(1)} %bitcast.5, bf16[1024,128]{1,0:T(8,128)(2,1)S(1)} %copy-done), custom_call_target="tpu_custom_call" | custom-call | tf_op jit(solution)/shard_map/pallas_call | solution.py:374
  104.2 0.7 copy.8
  104.9 0.6 copy.9
  105.5 0.6 copy.10
Async XLA Ops:
  0.6 1.0 copy-start
  1.6 0.8 copy-start.1
